TPU v7x, 512 devices: a whole 4x8x8 slice. The times are simulated.
512 devices in a mesh: dp: 64 (over z, y), tensor: 8 (over x, core).
Axes of the slice: x: 4, y: 8, z: 8, core: 2. Of those that a mesh axis runs over, the one named last changes fastest.
Arguments:
- tool_len: int32 [512], P('dp'), may hold values from 1 to 32
- state_table: int32 [512, 32], replicated, may hold values from 0 to 511, as said below
- page_table: int32 [512, 8, 4], replicated, may hold values from 0 to 2047, as said below
- kda_pool: bfloat16 [32, 512, 128, 128], P('tensor', 'dp'), may hold values from -6 to 6
- latent_pool: bfloat16 [8, 2048, 32, 512], P('tensor', 'dp'), may hold values from -6 to 6
- kda_q: bfloat16 [512, 32, 4096], P('dp', None, 'tensor'), may hold values from -6 to 6
- kda_k: bfloat16 [512, 32, 4096], P('dp', None, 'tensor'), may hold values from -6 to 6
- kda_v: bfloat16 [512, 32, 4096], P('dp', None, 'tensor'), may hold values from -6 to 6
- kda_gate: bfloat16 [512, 32, 4096], P('dp', None, 'tensor'), may hold values from -1.2 to 0
- kda_beta: bfloat16 [512, 32, 32], P('dp', None, 'tensor'), may hold values from -6 to 6
- mla_q: bfloat16 [512, 32, 4096], P('dp', None, 'tensor'), may hold values from -384 to 384
- mla_new: bfloat16 [512, 32, 512], P('dp'), may hold values from -6 to 6
- w_uk: bfloat16 [32, 128, 512], P('tensor'), may hold values from -0.5 to 0.5
- w_uv: bfloat16 [32, 512, 128], P('tensor'), may hold values from -0.25 to 0.25
Outputs:
- gated_recall_output: bfloat16 [512, 32, 4096], P('dp', None, 'tensor')
- mla_out: bfloat16 [512, 32, 4096], P('dp', None, 'tensor')
Inputs may be any that keep to these rules, and one draw needn't show every extreme that they name: `state_table`: for each head, every slot of its pool is named by exactly one row. For every index g of tensor, the records that the rows of one index of dp need in class g (their states of heads g * 4 to (g + 1) * 4 - 1 and their pages of class g) and that lie in the pools of one index of dp number at most 2, and exactly 2 for some pairs. `page_table`: for each class, every slot of its pool is named by exactly one page of one row; counted together with state_table as stated there.
All inputs are finite; a program needn't handle non-finite values.
Results may differ from a plain program's by a relative error of at most 0.015.
The roundings to bfloat16 on the way count: a program that leaves them out, or rounds other values in their place, can miss the bound.
Values may be sent and summed in bfloat16 or wider, within the bound.
A program may use at most 64 MiB of HBM per device.

v0:
```python
import jax
import jax.numpy as jnp
from jax import lax
from jax.sharding import PartitionSpec as P

EPSILON = 1e-06
HIGHEST = lax.Precision.HIGHEST


def unit_norm(values):
    return values / jnp.sqrt(jnp.sum(values * values, axis=-1, keepdims=True) + EPSILON)


def unit_sources(state_block, page_block):
    group_count, sequences_per_device, heads_dev = state_block.shape
    pages_row = page_block.shape[2]
    pool_pages = sequences_per_device * pages_row
    head_index = lax.broadcasted_iota(jnp.int32, state_block.shape, 2)
    state_owner = state_block // sequences_per_device
    state_record = head_index * sequences_per_device + state_block % sequences_per_device
    page_owner = page_block // pool_pages
    page_record = heads_dev * sequences_per_device + page_block % pool_pages
    owners = jnp.concatenate(
        [state_owner.reshape(group_count, -1), page_owner.reshape(group_count, -1)], axis=1
    )
    sources = jnp.concatenate(
        [state_record.reshape(group_count, -1), page_record.reshape(group_count, -1)], axis=1
    )
    return (owners, sources)


def kda_blocks(queries, keys_unit, values, betas, log_decay, initial):
    tokens_row = queries.shape[1]
    summed = jnp.cumsum(log_decay, axis=1)
    grown = jnp.exp(summed)
    shrunk = jnp.exp(-summed)
    query_up = queries * grown
    key_up = keys_unit * grown
    key_down = keys_unit * shrunk
    later = lax.broadcasted_iota(jnp.int32, (tokens_row, tokens_row), 0)
    sooner = lax.broadcasted_iota(jnp.int32, (tokens_row, tokens_row), 1)
    mixing = jnp.einsum("rthc,rshc->rhts", key_up, key_down, precision=HIGHEST)
    mixing = jnp.where(sooner < later, mixing, 0.0) * jnp.transpose(betas, (0, 2, 1))[..., None]
    system = mixing + jnp.eye(tokens_row, dtype=jnp.float32)
    target = betas[..., None] * (
        values - jnp.einsum("rthc,rhcd->rthd", key_up, initial, precision=HIGHEST)
    )
    target = jnp.transpose(target, (0, 2, 1, 3))
    updates = lax.linalg.triangular_solve(
        system, target, left_side=True, lower=True, unit_diagonal=True
    )
    reach = jnp.einsum("rthc,rshc->rhts", query_up, key_down, precision=HIGHEST)
    reach = jnp.where(sooner <= later, reach, 0.0)
    result = jnp.einsum("rthc,rhcd->rhtd", query_up, initial, precision=HIGHEST)
    result = result + jnp.einsum("rhts,rhsd->rhtd", reach, updates, precision=HIGHEST)
    return jnp.transpose(result, (0, 2, 1, 3))


def local(
    tool_len,
    state_table,
    page_table,
    kda_pool,
    latent_pool,
    kda_q,
    kda_k,
    kda_v,
    kda_gate,
    kda_beta,
    mla_q,
    mla_new,
    w_uk,
    w_uv,
):
    sequences_per_device = tool_len.shape[0]
    heads_dev = kda_pool.shape[0]
    head_dim = kda_pool.shape[2]
    page_len = latent_pool.shape[2]
    latent = latent_pool.shape[3]
    pages_row = page_table.shape[2]
    tokens_row = kda_q.shape[1]
    devices = lax.axis_size("dp")
    units = sequences_per_device * (heads_dev + pages_row)
    capacity = 2 * units // devices
    my_index = lax.axis_index("dp")
    tensor_index = lax.axis_index("tensor")
    state_group = lax.dynamic_slice_in_dim(state_table, tensor_index * heads_dev, heads_dev, 1)
    page_group = lax.dynamic_index_in_dim(page_table, tensor_index, 1, keepdims=False)
    owners, sources = unit_sources(
        state_group.reshape(devices, sequences_per_device, heads_dev),
        page_group.reshape(devices, sequences_per_device, pages_row),
    )
    mine = owners == my_index
    order = jnp.cumsum(mine.astype(jnp.int32), axis=1) - 1
    slot_ids = lax.broadcasted_iota(jnp.int32, (1, capacity, 1), 1)
    matches = mine[:, None, :] & (order[:, None, :] == slot_ids)
    picked = jnp.sum(jnp.where(matches, sources[:, None, :], 0), axis=2)
    filled = jnp.any(matches, axis=2)
    records = jnp.concatenate(
        [kda_pool.reshape(heads_dev * sequences_per_device, page_len, latent), latent_pool[0]],
        axis=0,
    )
    outgoing = jnp.take(records, picked.reshape(-1), axis=0).reshape(
        devices, capacity, page_len, latent
    )
    outgoing = jnp.where(filled[:, :, None, None], outgoing, jnp.zeros((), outgoing.dtype))
    incoming = lax.all_to_all(outgoing, "dp", split_axis=0, concat_axis=0, tiled=True)
    own_owners = lax.dynamic_index_in_dim(owners, my_index, 0, keepdims=False)
    position = lax.broadcasted_iota(jnp.int32, (units, units), 0)
    other_pos = lax.broadcasted_iota(jnp.int32, (units, units), 1)
    before = (own_owners[None, :] == own_owners[:, None]) & (other_pos < position)
    ranks = jnp.sum(before.astype(jnp.int32), axis=1)
    fetched = jnp.take(
        incoming.reshape(devices * capacity, page_len, latent),
        own_owners * capacity + ranks,
        axis=0,
    )
    states = (
        fetched[: sequences_per_device * heads_dev]
        .reshape(sequences_per_device, heads_dev, head_dim, head_dim)
        .astype(jnp.float32)
    )
    pages = fetched[sequences_per_device * heads_dev :].reshape(
        sequences_per_device, pages_row * page_len, latent
    )
    alive = (
        lax.broadcasted_iota(jnp.int32, (sequences_per_device, tokens_row), 1) < tool_len[:, None]
    )
    alive_f = alive.astype(jnp.float32)

    def per_head(values):
        return values.reshape(sequences_per_device, tokens_row, heads_dev, head_dim)

    query_n = unit_norm(per_head(kda_q).astype(jnp.float32))
    key_n = unit_norm(per_head(kda_k).astype(jnp.float32))
    value_f = per_head(kda_v).astype(jnp.float32)
    betas = jax.nn.sigmoid(kda_beta.astype(jnp.float32)) * alive_f[:, :, None]
    log_decay = per_head(kda_gate).astype(jnp.float32) * alive_f[:, :, None, None]
    delta_layer_result = kda_blocks(query_n, key_n, value_f, betas, log_decay, states)
    gated_recall_output = (
        (delta_layer_result * alive_f[:, :, None, None])
        .reshape(sequences_per_device, tokens_row, heads_dev * head_dim)
        .astype(jnp.bfloat16)
    )
    lifted = jnp.einsum(
        "rthd,hdl->rthl", per_head(mla_q), w_uk, preferred_element_type=jnp.float32
    ).astype(jnp.bfloat16)
    scale = head_dim ** (-0.5)
    later = lax.broadcasted_iota(jnp.int32, (tokens_row, tokens_row), 0)
    sooner = lax.broadcasted_iota(jnp.int32, (tokens_row, tokens_row), 1)
    causal = (sooner <= later)[None, :, None, :]
    new_scores = (
        jnp.einsum("rthl,rsl->rths", lifted, mla_new, preferred_element_type=jnp.float32) * scale
    )
    new_scores = jnp.where(causal, new_scores, -1e30)
    context = lax.all_gather(pages, "tensor", axis=1, tiled=True)
    old_scores = (
        jnp.einsum("rthl,rcl->rthc", lifted, context, preferred_element_type=jnp.float32) * scale
    )
    top = jnp.maximum(jnp.max(old_scores, axis=-1), jnp.max(new_scores, axis=-1))
    old_e = jnp.exp(old_scores - top[..., None])
    new_e = jnp.where(causal, jnp.exp(new_scores - top[..., None]), 0.0)
    totals = jnp.sum(old_e, axis=-1) + jnp.sum(new_e, axis=-1)
    old_weights = old_e.astype(jnp.bfloat16)
    new_weights = new_e.astype(jnp.bfloat16)
    fresh_part = jnp.einsum(
        "rths,rsl->rthl", new_weights, mla_new, preferred_element_type=jnp.float32
    )
    mixed = fresh_part + jnp.einsum(
        "rthc,rcl->rthl", old_weights, context, preferred_element_type=jnp.float32
    )
    attended = (mixed / totals[..., None]).astype(jnp.bfloat16)
    mla_result = jnp.einsum("rthl,hld->rthd", attended, w_uv, preferred_element_type=jnp.float32)
    mla_out = (
        (mla_result * alive_f[:, :, None, None])
        .reshape(sequences_per_device, tokens_row, heads_dev * head_dim)
        .astype(jnp.bfloat16)
    )
    return (gated_recall_output, mla_out)


def solution(mesh):
    in_specs = (
        P("dp"),
        P(),
        P(),
        P("tensor", "dp", None, None),
        P("tensor", "dp", None, None),
        P("dp", None, "tensor"),
        P("dp", None, "tensor"),
        P("dp", None, "tensor"),
        P("dp", None, "tensor"),
        P("dp", None, "tensor"),
        P("dp", None, "tensor"),
        P("dp", None, None),
        P("tensor", None, None),
        P("tensor", None, None),
    )
    out_specs = (P("dp", None, "tensor"), P("dp", None, "tensor"))
    return jax.shard_map(local, mesh=mesh, in_specs=in_specs, out_specs=out_specs, check_vma=False)
```

profile of v0, /device:TPU:42, one launch (start us, length us, event | category | flops | bytes accessed | tf_op | source)
XLA Modules:
  0.0 289.8 jit_solution(12379992508543004669)
XLA Ops:
  7.3 0.8 constant_dynamic-slice_fusion
  8.4 0.7 constant_dynamic-slice_fusion.1
  10.7 1.4 reshape.251
  12.1 1.7 pad_maximum_fusion
  13.8 2.8 gather_fusion
  16.6 3.9 %select_select_fusion = bf16[64,2,32,512]{3,2,1,0:T(8,128)(2,1)} fusion(bf16[64,2,32,512]{3,2,1,0:T(8,128)(2,1)} %bitcast.102, pred[64,2]{1,0:T(8,128)(4,1)S(1)} %copy.127, pred[64,2]{1,0:T(8,128)(4,1)S(1)} %copy.126), kind=kLoop, calls=%fused_computation.7 | loop fusion | flops 4194304 | bytes 8388864 | tf_op jit(solution)/shard_map/jit(_where)/select_n | solution.py:106
  20.5 16.3 %all-to-all-start = ((bf16[64,2,32,512]{3,2,1,0:T(8,128)(2,1)}), bf16[64,2,32,512]{3,2,1,0:T(8,128)(2,1)}, u32[]{:S(2)}, u32[]{:S(2)}) async-start(bf16[64,2,32,512]{3,2,1,0:T(8,128)(2,1)} %select_select_fusion), calls=%async_computation | async-start | bytes 8388608 | tf_op jit(solution)/shard_map/all_to_all | solution.py:107
  37.1 127.6 %all-to-all-done = bf16[64,2,32,512]{3,2,1,0:T(8,128)(2,1)} async-done(((bf16[64,2,32,512]{3,2,1,0:T(8,128)(2,1)}), bf16[64,2,32,512]{3,2,1,0:T(8,128)(2,1)}, u32[]{:S(2)}, u32[]{:S(2)}) %all-to-all-start) | async-done | bytes 4194336 | tf_op jit(solution)/shard_map/all_to_all | solution.py:107
  164.8 2.9 gather_fusion.1
  168.0 1.5 fusion.61
  169.7 0.7 copy.122
  170.5 0.3 multiply_reduce_fusion.2
  171.3 0.3 multiply_reduce_fusion.1
  171.9 1.0 reshape.258
  173.0 1.9 exponential_multiply_fusion.1
  174.9 1.1 fusion.14
  176.0 79.7 %custom-call.3 = f32[8,4,1,32,32]{3,4,2,1,0:T(8,128)} custom-call(f32[8,4,1,32,32]{4,3,2,1,0:T(8,128)S(1)} %fusion.14), custom_call_target="InvertDiagBlocksLowerTriangular" | custom-call | tf_op jit(solution)/shard_map/triangular_solve | solution.py:49
  255.7 1.3 divide_multiply_fusion
  257.1 1.9 convolution_select_fusion.1
  258.9 0.4 fusion.64
  259.4 1.7 fusion.62
  261.1 2.5 reshape.254
  263.6 2.4 fusion.17
  266.0 1.0 fusion.27
  267.1 0.7 fusion.63
  267.7 0.9 fusion.21
  268.7 0.7 copy.201
  269.4 6.4 %multiply_reduce_fusion = (f32[8,32,4]{1,2,0:T(4,128)S(1)}, f32[8,32,4,1024]{3,1,2,0:T(8,128)S(1)}) fusion(bf16[8,1024,512]{2,1,0:T(8,128)(2,1)} %all-gather.2.cloned.1.call-done, f32[4,512,8,32]{1,3,2,0:T(8,128)S(1)} %bitcast.101), kind=kOutput, calls=%fused_computation.8 | convolution fusion | flops 1076362240 | bytes 14684160 | tf_op jit(solution)/shard_map/rthl,rcl->rthc/dot_general | solution.py:158
  275.9 1.0 fusion.4
  277.2 2.6 fusion.2
  279.8 2.4 fusion.22
  282.2 0.8 copy.200
  (88 shorter events, 3.8 us)
Async XLA Ops:
  7.2 251.8 %copy-start = (bf16[4,128,512]{2,1,0:T(8,128)(2,1)S(1)}, bf16[4,128,512]{2,1,0:T(8,128)(2,1)}, u32[]{:S(2)}) copy-start(bf16[4,128,512]{2,1,0:T(8,128)(2,1)} %param.26) | copy-start | bytes 1572868
  7.2 3.5 %copy-start.6 = (bf16[4,8,128,128]{3,2,1,0:T(8,128)(2,1)S(1)}, bf16[4,8,128,128]{3,2,1,0:T(8,128)(2,1)}, u32[]{:S(2)}) copy-start(bf16[4,8,128,128]{3,2,1,0:T(8,128)(2,1)} %param.17) | copy-start | bytes 3145732
  20.5 144.3 %all-to-all-start = ((bf16[64,2,32,512]{3,2,1,0:T(8,128)(2,1)}), bf16[64,2,32,512]{3,2,1,0:T(8,128)(2,1)}, u32[]{:S(2)}, u32[]{:S(2)}) async-start(bf16[64,2,32,512]{3,2,1,0:T(8,128)(2,1)} %select_select_fusion), calls=%async_computation | async-start | bytes 8388608 | tf_op jit(solution)/shard_map/all_to_all | solution.py:107
  36.8 232.6 %all-gather.2.cloned.1.call-start = ((), (), s32[]{:S(2)}) async-start(), calls=%async_computation.1 | async-start | bytes 9437184 | tf_op jit(solution)/shard_map/all_gather | solution.py:156
  167.9 1.7 copy-start.17
  168.0 2.4 copy-start.8
  169.5 1.6 copy-start.9
  169.5 2.4 copy-start.10
  170.4 2.6 copy-start.16
  173.0 84.0 %copy-start.12 = (bf16[8,32,512]{2,1,0:T(8,128)(2,1)S(1)}, bf16[8,32,512]{2,1,0:T(8,128)(2,1)}, u32[]{:S(2)}) copy-start(bf16[8,32,512]{2,1,0:T(8,128)(2,1)} %param.24) | copy-start | bytes 786436
  174.9 84.0 %copy-start.3 = (f32[8,32,4,128]{3,0,1,2:T(8,128)}, f32[8,32,4,128]{3,0,1,2:T(8,128)S(1)}, u32[]{:S(2)}) copy-start(f32[8,32,4,128]{3,0,1,2:T(8,128)S(1)} %get-tuple-element.8) | copy-start | bytes 1572868
  257.0 2.3 copy-start.13
  259.4 4.2 %copy-start.11 = (bf16[8,32,512]{2,1,0:T(8,128)(2,1)S(1)}, bf16[8,32,512]{2,1,0:T(8,128)(2,1)}, u32[]{:S(2)}) copy-start(bf16[8,32,512]{2,1,0:T(8,128)(2,1)} %param.21) | copy-start | bytes 786436
  259.4 4.2 %copy-start.15 = (f32[8,32,4]{1,2,0:T(4,128)S(1)}, f32[8,32,4]{1,2,0:T(4,128)}, u32[]{:S(2)}) copy-start(f32[8,32,4]{1,2,0:T(4,128)} %divide_multiply_fusion) | copy-start | bytes 12292
  263.6 2.4 copy-start.7
  263.6 3.4 %copy-start.4 = (f32[8,4,32,32]{3,2,1,0:T(8,128)S(1)}, f32[8,4,32,32]{3,2,1,0:T(8,128)}, u32[]{:S(2)}) copy-start(f32[8,4,32,32]{3,2,1,0:T(8,128)} %convolution_select_fusion.1) | copy-start | bytes 393220
  266.0 1.7 copy-start.1
  269.4 7.7 %copy-start.2 = (bf16[8,1024,512]{2,1,0:T(8,128)(2,1)S(1)}, bf16[8,1024,512]{2,1,0:T(8,128)(2,1)}, u32[]{:S(2)}) copy-start(bf16[8,1024,512]{2,1,0:T(8,128)(2,1)} %all-gather.2.cloned.1.call-done) | copy-start | bytes 25165828
  275.9 1.0 copy-start.5
  277.1 2.6 copy-start.14
  277.1 2.6 copy-start.18
Sparse Core Ops, SparseCore 0:
  169.6 51.3 all-gather.1
where the time goes:
time: 290 us
  waiting for transfers between devices  128 us (44%)
  other arithmetic  91.9 us (32%)
  matrix products  21.6 us (7%)
  local copies, waits for them, and re-layouts  17.9 us (6%)
  starting transfers between devices  16.4 us (6%)
  between operations  14.5 us (5%)
    all_to_all x1, waiting for transfers between devices, local(): lax.all_to_all(outgoing, 'dp', split_axis=0, concat_axis=0, tiled=True)  128 us
    another operation x2, other arithmetic, kda_blocks(): lax.linalg.triangular_solve(system, target, left_side=True, lower=True, u...  79.7 us
    all_to_all x1, starting transfers between devices, local(): lax.all_to_all(outgoing, 'dp', split_axis=0, concat_axis=0, tiled=True)  16.3 us
    dot_general x1, matrix products, local(): jnp.einsum('rthl,rcl->rthc', lifted, context, preferred_element_type=jnp....  6.45 us
  transfers between devices with their start and end apart: 2, of which 1 were waited for; matrix products, arithmetic and copies ran while one was open for 34% of the time, Pallas kernels for 0%

commit v1 on v0

v1 whole, which is shorter than its diff:
```python
import functools

import jax
import jax.numpy as jnp
from jax import lax
from jax.experimental import pallas as pl
from jax.experimental.pallas import tpu as pltpu
from jax.sharding import PartitionSpec as P

EPSILON = 1e-06
F32 = jnp.float32
BF16 = jnp.bfloat16


def mm(a, b):
    return lax.dot_general(a, b, (((1,), (0,)), ((), ())), preferred_element_type=F32)


def mm_nt(a, b):
    return lax.dot_general(a, b, (((1,), (1,)), ((), ())), preferred_element_type=F32)


def halves(values):
    high = values.astype(BF16)
    return high, (values - high.astype(F32)).astype(BF16)


def mm3(a, b, dot=mm):
    a_high, a_low = halves(a)
    b_high, b_low = halves(b)
    return dot(a_high, b_high) + (dot(a_high, b_low) + dot(a_low, b_high))


def unit_norm(values):
    return values / jnp.sqrt(jnp.sum(values * values, axis=-1, keepdims=True) + EPSILON)


def stack_heads(block, heads, width):
    return jnp.concatenate([block[:, h * width : (h + 1) * width] for h in range(heads)], axis=0)


def recall_coefficients(queries, keys, values, gates, betas, alive, tokens):
    rows = queries.shape[0]
    later = lax.broadcasted_iota(jnp.int32, (rows, rows), 0)
    sooner = lax.broadcasted_iota(jnp.int32, (rows, rows), 1)
    same = (later // tokens) == (sooner // tokens)
    reached = same & (sooner <= later)
    summed = mm(reached.astype(F32).astype(BF16), (gates.astype(F32) * alive).astype(BF16))
    grown = jnp.exp(summed)
    key_n = unit_norm(keys.astype(F32))
    query_up = unit_norm(queries.astype(F32)) * grown
    key_up = key_n * grown
    key_down = key_n * jnp.exp(-summed)
    mixing = mm3(key_up, key_down, mm_nt) * betas
    reach = jnp.where(reached, mm3(query_up, key_down, mm_nt), 0.0)
    inverse = (later == sooner).astype(F32)
    size = 1
    while size < tokens:
        pair = 2 * size
        corner = ((later // pair) == (sooner // pair)) & (later % pair >= size) & (sooner % pair < size)
        part = jnp.where(corner, mixing, 0.0)
        if size == 1:
            inverse = inverse - part
        else:
            inverse = inverse - mm3(mm3(inverse, part), inverse)
        size = pair
    spread = mm3(reach, inverse)
    coefficient = query_up - mm3(spread, betas * key_up)
    offset = mm3(spread, betas * values.astype(F32))
    return coefficient, offset


def fused(
    sizes,
    picked_ref,
    slot_ref,
    len_ref,
    states_ref,
    pages_ref,
    q_ref,
    k_ref,
    v_ref,
    gate_ref,
    beta_ref,
    mq_ref,
    new_ref,
    wuk_ref,
    wuv_ref,
    recall_ref,
    mla_ref,
    records,
    outgoing,
    incoming,
    lift_out,
    lift_in,
    wuv_in,
    page_out,
    context,
    result_out,
    coefs,
    offsets,
    x_send_sem,
    x_recv_sem,
    swap_send_sem,
    swap_recv_sem,
    lift_send_sem,
    lift_recv_sem,
    wuv_send_sem,
    wuv_recv_sem,
    back_send_sem,
    back_recv_sem,
):
    n_dp, n_t, cap = sizes
    heads, slots, hd, _ = states_ref.shape
    page_len, latent = pages_ref.shape[2], pages_ref.shape[3]
    rows, tokens, _ = q_ref.shape
    folds = latent // hd
    me = lax.axis_index("dp")
    mine = lax.axis_index("tensor")

    barrier = pltpu.get_barrier_semaphore()

    def greet_dp(k, c):
        pl.semaphore_signal(barrier, inc=1, device_id={"dp": (me + k) % n_dp})
        return c

    def greet_tensor(k, c):
        pl.semaphore_signal(barrier, inc=1, device_id={"tensor": (mine + k) % n_t})
        return c

    lax.fori_loop(1, n_dp, greet_dp, 0)
    lax.fori_loop(1, n_t, greet_tensor, 0)

    def put_state(i, c):
        records[i] = states_ref[i // slots, i % slots]
        return c

    def put_page(i, c):
        page = pages_ref[0, i]
        for f in range(folds):
            records[heads * slots + i, f * page_len : (f + 1) * page_len, :] = page[
                :, f * hd : (f + 1) * hd
            ]
        return c

    lax.fori_loop(0, heads * slots, put_state, 0)
    lax.fori_loop(0, pages_ref.shape[1], put_page, 0)
    for s in range(cap):
        incoming[me * cap + s] = records[picked_ref[me * cap + s]]

    pl.semaphore_wait(barrier, n_dp + n_t - 2)

    def send_records(k, c):
        peer = (me + (k * 27) % n_dp) % n_dp
        for s in range(cap):
            outgoing[peer * cap + s] = records[picked_ref[peer * cap + s]]
        pltpu.make_async_remote_copy(
            src_ref=outgoing.at[pl.ds(peer * cap, cap)],
            dst_ref=incoming.at[pl.ds(me * cap, cap)],
            send_sem=x_send_sem,
            recv_sem=x_recv_sem,
            device_id={"dp": peer},
        ).start()
        return c

    lax.fori_loop(1, n_dp, send_records, 0)

    for h in range(heads):
        queries = mq_ref[:, :, h * hd : (h + 1) * hd].reshape(rows * tokens, hd)
        lifted = mm(queries, wuk_ref[h]).astype(BF16)
        lift_out[:, h] = lifted.reshape(rows, tokens, latent)
    lift_in[0] = lift_out[mine]
    wuv_in[0] = wuv_ref[...]

    def lift_copy(k):
        peer = (mine + k) % n_t
        return pltpu.make_async_remote_copy(
            src_ref=lift_out.at[peer],
            dst_ref=lift_in.at[n_t - k],
            send_sem=lift_send_sem.at[k],
            recv_sem=lift_recv_sem.at[n_t - k],
            device_id={"tensor": peer},
        )

    def wuv_copy(k):
        peer = (mine + k) % n_t
        return pltpu.make_async_remote_copy(
            src_ref=wuv_ref,
            dst_ref=wuv_in.at[n_t - k],
            send_sem=wuv_send_sem.at[k],
            recv_sem=wuv_recv_sem.at[n_t - k],
            device_id={"tensor": peer},
        )

    def page_copy(k):
        peer = (mine + k) % n_t
        return pltpu.make_async_remote_copy(
            src_ref=page_out.at[peer],
            dst_ref=context.at[n_t - k],
            send_sem=swap_send_sem.at[k],
            recv_sem=swap_recv_sem.at[n_t - k],
            device_id={"tensor": peer},
        )

    def back_copy(k):
        peer = (mine + k) % n_t
        return pltpu.make_async_remote_copy(
            src_ref=result_out.at[k],
            dst_ref=mla_ref.at[mine],
            send_sem=back_send_sem.at[k],
            recv_sem=back_recv_sem.at[n_t - k],
            device_id={"tensor": peer},
        )

    for k in range(1, n_t):
        lift_copy(k).start()
    for k in range(1, n_t):
        wuv_copy(k).start()

    def make_coefficients(r, c):
        alive = (
            lax.broadcasted_iota(jnp.int32, (heads * tokens, 1), 0) % tokens < len_ref[r]
        ).astype(F32)
        raw = beta_ref[r].astype(F32)
        betas = jnp.concatenate([raw[:, h : h + 1] for h in range(heads)], axis=0)
        betas = alive / (1.0 + jnp.exp(-betas))
        coefficient, offset = recall_coefficients(
            stack_heads(q_ref[r], heads, hd),
            stack_heads(k_ref[r], heads, hd),
            stack_heads(v_ref[r], heads, hd),
            stack_heads(gate_ref[r], heads, hd),
            betas,
            alive,
            tokens,
        )
        coefs[r] = coefficient
        offsets[r] = offset
        return c

    lax.fori_loop(0, rows, make_coefficients, 0)

    fresh = new_ref[mine]
    context[n_t] = jnp.concatenate(
        [fresh, jnp.zeros((context.shape[1] - tokens, latent), BF16)], axis=0
    )

    away = (n_dp - 1) * cap
    pltpu.make_async_copy(
        incoming.at[pl.ds(0, away)], incoming.at[pl.ds(0, away)], x_recv_sem
    ).wait()

    n_states = heads * rows

    def place_page(i, c):
        record = incoming[slot_ref[n_states + i]]
        for f in range(folds):
            page_out[
                i // pages_row,
                pl.ds((i % pages_row) * page_len, page_len),
                f * hd : (f + 1) * hd,
            ] = record[f * page_len : (f + 1) * page_len]
        return c

    pages_row = page_out.shape[1] // page_len
    lax.fori_loop(0, rows * pages_row, place_page, 0)
    context[0] = page_out[mine]
    for k in range(1, n_t):
        page_copy(k).start()

    def recall(r, c):
        alive = (lax.broadcasted_iota(jnp.int32, (tokens, 1), 0) < len_ref[r]).astype(F32)
        for h in range(heads):
            state = incoming[slot_ref[h * rows + r]]
            high, low = halves(coefs[r, h * tokens : (h + 1) * tokens, :])
            both = mm(jnp.concatenate([high, low], axis=0), state)
            seen = both[:tokens] + both[tokens:] + offsets[r, h * tokens : (h + 1) * tokens, :]
            recall_ref[r, :, h * hd : (h + 1) * hd] = (seen * alive).astype(BF16)
        return c

    lax.fori_loop(0, rows, recall, 0)

    for k in range(1, n_t):
        lift_copy(k).wait_recv()
        wuv_copy(k).wait_recv()
    for k in range(1, n_t):
        page_copy(k).wait_recv()

    every = heads * tokens
    scale = hd ** (-0.5)
    total_keys = context.shape[0] * context.shape[1]
    old_keys = n_t * context.shape[1]
    column = lax.broadcasted_iota(jnp.int32, (every, total_keys), 1) - old_keys
    token = lax.broadcasted_iota(jnp.int32, (every, total_keys), 0) % tokens
    row_alive = (lax.broadcasted_iota(jnp.int32, (tokens, 1), 0) < len_ref[mine]).astype(F32)

    def attend(k):
        keys = context[...].reshape(total_keys, latent)
        queries = lift_in[k].reshape(every, latent)
        scores = mm_nt(queries, keys) * scale
        scores = jnp.where(column <= token, scores, -1e30)
        top = jnp.max(scores, axis=-1, keepdims=True)
        e = jnp.exp(scores - top)
        total = jnp.sum(e, axis=-1, keepdims=True)
        mixed = mm(e.astype(BF16), keys)
        attended = (mixed / total).astype(BF16)
        for h in range(heads):
            out = mm(attended[h * tokens : (h + 1) * tokens], wuv_in[k, h]) * row_alive
            result_out[k, :, h * hd : (h + 1) * hd] = out.astype(BF16)

    def attend_away(k, c):
        attend(k)
        back_copy(k).start()
        return c

    lax.fori_loop(1, n_t, attend_away, 0)
    attend(0)
    mla_ref[mine] = result_out[0]

    for k in range(1, n_t):
        back_copy(k).wait_recv()
    for k in range(1, n_t):
        lift_copy(k).wait_send()
        wuv_copy(k).wait_send()
        page_copy(k).wait_send()
        back_copy(k).wait_send()
    pltpu.make_async_copy(
        outgoing.at[pl.ds(0, away)], outgoing.at[pl.ds(0, away)], x_send_sem
    ).wait()


def run_fused(
    n_dp,
    n_t,
    cap,
    picked,
    slot,
    tool_len,
    kda_pool,
    latent_pool,
    kda_q,
    kda_k,
    kda_v,
    kda_gate,
    kda_beta,
    mla_q,
    mla_new,
    w_uk,
    w_uv,
):
    heads, slots, hd, _ = kda_pool.shape
    _, pool_pages, page_len, latent = latent_pool.shape
    rows, tokens, _ = kda_q.shape
    pages_row = pool_pages // rows
    vmem = pl.BlockSpec(memory_space=pltpu.VMEM)
    smem = pl.BlockSpec(memory_space=pltpu.SMEM)
    out = jax.ShapeDtypeStruct(kda_q.shape, BF16)
    dma = pltpu.SemaphoreType.DMA
    return pl.pallas_call(
        functools.partial(fused, (n_dp, n_t, cap)),
        out_shape=(out, out),
        in_specs=[smem] * 3 + [vmem] * 11,
        out_specs=(vmem, vmem),
        scratch_shapes=[
            pltpu.VMEM((heads * slots + pool_pages, hd, hd), BF16),
            pltpu.VMEM((n_dp * cap, hd, hd), BF16),
            pltpu.VMEM((n_dp * cap, hd, hd), BF16),
            pltpu.VMEM((rows, heads, tokens, latent), BF16),
            pltpu.VMEM((n_t, heads, tokens, latent), BF16),
            pltpu.VMEM((n_t, heads, latent, hd), BF16),
            pltpu.VMEM((rows, pages_row * page_len, latent), BF16),
            pltpu.VMEM((n_t + 1, pages_row * page_len, latent), BF16),
            pltpu.VMEM((n_t, tokens, heads * hd), BF16),
            pltpu.VMEM((rows, heads * tokens, hd), F32),
            pltpu.VMEM((rows, heads * tokens, hd), F32),
            dma,
            dma,
        ]
        + [dma((n_t,))] * 8,
        compiler_params=pltpu.CompilerParams(
            collective_id=0, has_side_effects=True, vmem_limit_bytes=48 * 1024 * 1024
        ),
    )(
        picked,
        slot,
        tool_len,
        kda_pool,
        latent_pool,
        kda_q,
        kda_k,
        kda_v,
        kda_gate,
        kda_beta,
        mla_q,
        mla_new,
        w_uk,
        w_uv,
    )


def routes(state_table, page_table, n_dp, heads, rows, pool_pages):
    me = lax.axis_index("dp")
    mine = lax.axis_index("tensor")
    pages_row = page_table.shape[2]
    states = lax.dynamic_slice_in_dim(state_table, mine * heads, heads, 1).T
    pages = lax.dynamic_index_in_dim(page_table, mine, 1, keepdims=False).T
    owners = jnp.concatenate([states // rows, pages // pool_pages], axis=0)
    head = lax.broadcasted_iota(jnp.int32, states.shape, 0)
    ids = jnp.concatenate([head * rows + states % rows, heads * rows + pages % pool_pages], axis=0)
    kinds = heads + pages_row
    here = (owners == me).reshape(kinds, n_dp, rows)
    ids3 = ids.reshape(kinds, n_dp, rows)
    top = heads * rows + pool_pages - 1
    first = jnp.min(jnp.where(here, ids3, top), axis=(0, 2))
    second = jnp.max(jnp.where(here, ids3, 0), axis=(0, 2))
    picked = jnp.stack([first, second], axis=1).reshape(-1)
    own = lax.dynamic_slice_in_dim(owners, me * rows, rows, 1)
    own_ids = lax.dynamic_slice_in_dim(ids, me * rows, rows, 1)
    own = jnp.concatenate([own[:heads].reshape(-1), own[heads:].T.reshape(-1)])
    own_ids = jnp.concatenate([own_ids[:heads].reshape(-1), own_ids[heads:].T.reshape(-1)])
    behind = (own[None, :] == own[:, None]) & (own_ids[None, :] < own_ids[:, None])
    slot = 2 * own + jnp.any(behind, axis=1).astype(jnp.int32)
    return picked, slot


def local(
    tool_len,
    state_table,
    page_table,
    kda_pool,
    latent_pool,
    kda_q,
    kda_k,
    kda_v,
    kda_gate,
    kda_beta,
    mla_q,
    mla_new,
    w_uk,
    w_uv,
):
    n_dp, n_t = lax.axis_size("dp"), lax.axis_size("tensor")
    picked, slot = routes(
        state_table, page_table, n_dp, kda_pool.shape[0], tool_len.shape[0], latent_pool.shape[1]
    )
    return run_fused(
        n_dp,
        n_t,
        2,
        picked,
        slot,
        tool_len,
        kda_pool,
        latent_pool,
        kda_q,
        kda_k,
        kda_v,
        kda_gate,
        kda_beta,
        mla_q,
        mla_new,
        w_uk,
        w_uv,
    )


def solution(mesh):
    in_specs = (
        P("dp"),
        P(),
        P(),
        P("tensor", "dp", None, None),
        P("tensor", "dp", None, None),
        P("dp", None, "tensor"),
        P("dp", None, "tensor"),
        P("dp", None, "tensor"),
        P("dp", None, "tensor"),
        P("dp", None, "tensor"),
        P("dp", None, "tensor"),
        P("dp", None, None),
        P("tensor", None, None),
        P("tensor", None, None),
    )
    out_specs = (P("dp", None, "tensor"), P("dp", None, "tensor"))
    return jax.shard_map(local, mesh=mesh, in_specs=in_specs, out_specs=out_specs, check_vma=False)
```

time: 290 us -> 186 us (0.64)
  the two profiles are of different devices: /device:TPU:42 before, /device:TPU:27 now
where the time goes in v1:
time: 186 us; the launch traced here: 185 us
  Pallas kernels  168 us (90%)
  local copies, waits for them, and re-layouts  12.4 us (7%)
  other arithmetic  3.73 us (2%)
    pallas_call x1, Pallas kernels, run_fused(): pl.pallas_call(functools.partial(fused, (n_dp, n_t, cap)), out_shape=(out...  168 us
    unnamed x25, local copies, waits for them, and re-layouts  11.4 us

profile of v1, /device:TPU:27, one launch (start us, length us, event | category | flops | bytes accessed | tf_op | source)
XLA Modules:
  0.0 185.1 jit_solution(17648145016875316564)
XLA Ops:
  0.7 0.8 fusion.1
  1.5 0.7 add_select_fusion.3
  2.2 0.7 fusion.2
  3.0 0.1 fusion.7
  3.0 0.1 reshape.40
  3.1 0.1 copy.26
  3.2 0.1 reshape.41
  3.3 0.7 add_select_fusion.2
  4.1 0.1 fusion.8
  4.1 0.1 reshape.38
  4.2 0.1 copy.25
  4.3 0.1 reshape.39
  4.5 0.2 and_reduce_fusion
  4.7 0.1 reduce_min.14
  4.8 0.1 reduce_min.18
  4.9 0.1 reduce_max.14
  5.0 0.1 reduce_max.18
  5.1 0.1 copy.24
  5.2 0.1 reshape.37.picked_ref
  5.4 0.8 copy.27.beta_ref
  6.2 1.2 copy-done
  7.5 1.2 copy-done.1
  8.7 1.0 copy-done.3
  9.7 0.9 copy-done.4
  10.7 0.9 copy-done.5
  11.6 0.9 copy-done.6
  12.6 0.9 copy-done.7
  13.5 0.9 copy-done.8
  14.5 0.9 copy-done.9
  15.4 168.3 %shard_map.149 = (bf16[8,32,512]{2,1,0:T(8,128)(2,1)S(1)}, bf16[8,32,512]{2,1,0:T(8,128)(2,1)S(1)}) custom-call(s32[128]{0:T(128)S(1)} %reshape.37.picked_ref, s32[64]{0:T(128)S(1)} %convert_add_fusion.slot_ref, s32[8]{0:T(128)S(1)} %copy-done.10, bf16[4,8,128,128]{3,2,1,0:T(8,128)(2,1)S(1)} %copy-done, bf16[1,32,32,512]{3,2,1,0:T(8,128)(2,1)S(1)} %copy-done.1, ...), custom_call_target="tpu_custom_call" | custom-call | tf_op jit(solution)/shard_map/pallas_call | solution.py:358
  183.7 0.7 copy.30
  184.4 0.7 copy.31
  (20 shorter events, 0.2 us)
Async XLA Ops:
  0.6 5.6 %copy-start.2 = (bf16[4,128,512]{2,1,0:T(8,128)(2,1)S(1)}, bf16[4,128,512]{2,1,0:T(8,128)(2,1)}, u32[]{:S(2)}) copy-start(bf16[4,128,512]{2,1,0:T(8,128)(2,1)} %wuk_ref.1) | copy-start | bytes 1572868
  5.4 0.9 copy-start.10
  6.2 1.2 copy-start
  7.5 1.2 copy-start.1
  8.7 1.0 copy-start.3
  9.7 0.9 copy-start.4
  10.7 0.9 copy-start.5
  11.6 0.9 copy-start.6
  12.6 0.9 copy-start.7
  13.5 0.9 copy-start.8
  14.5 0.9 copy-start.9

commit v2 on v1

--- a/solution.py
+++ b/solution.py
@@ -10,6 +10,8 @@
 EPSILON = 1e-06
 F32 = jnp.float32
 BF16 = jnp.bfloat16
+LANES = 128
+SIDE_Y = 8
 
 
 def mm(a, b):
@@ -70,11 +72,53 @@
     return coefficient, offset
 
 
+def routes(states, pages, me, side, rows, slots, pool_pages):
+    n_z, n_y = side
+    n_dp = n_z * n_y
+    heads = states.shape[0]
+    lanes = states.shape[1]
+    kinds = heads + pages.shape[0]
+    owners = jnp.concatenate([states // slots, pages // pool_pages], axis=0)
+    head = lax.broadcasted_iota(jnp.int32, states.shape, 0)
+    ids = jnp.concatenate(
+        [head * slots + states % slots, heads * slots + pages % pool_pages], axis=0
+    )
+    here = owners == me
+    first = jnp.min(jnp.where(here, ids, heads * slots + pool_pages - 1), axis=0, keepdims=True)
+    second = jnp.max(jnp.where(here, ids, 0), axis=0, keepdims=True)
+    span = 1
+    while span < rows:
+        first = jnp.minimum(first, pltpu.roll(first, lanes - span, 1))
+        second = jnp.maximum(second, pltpu.roll(second, lanes - span, 1))
+        span *= 2
+    keys = owners * (heads * slots + pool_pages) + ids
+    own = pltpu.roll(keys, (lanes - me * rows) % lanes, 1)[:, :LANES]
+    place = lax.broadcasted_iota(jnp.int32, (1, LANES), 1)
+    flat = jnp.zeros((1, LANES), jnp.int32)
+    for kind in range(kinds):
+        row = own[kind : kind + 1]
+        if kind:
+            row = pltpu.roll(row, kind * rows, 1)
+        flat = jnp.where(place // rows == kind, row, flat)
+    across = jnp.broadcast_to(flat, (LANES, LANES))
+    down = jnp.transpose(across.astype(F32)).astype(jnp.int32)
+    base = heads * slots + pool_pages
+    valid = lax.broadcasted_iota(jnp.int32, (LANES, LANES), 0) < kinds * rows
+    behind = valid & (down // base == across // base) & (down < across)
+    late = jnp.max(behind.astype(F32), axis=0, keepdims=True).astype(jnp.int32)
+    source = flat // base
+    over_z = (me // n_y - source // n_y + n_z) % n_z
+    over_y = (me % n_y - source % n_y + n_y) % n_y
+    by_z = jnp.where(over_y == 0, 0, n_dp) + over_z * n_y + over_y
+    by_y = jnp.where(over_z == 0, 0, n_dp) + over_y * n_z + over_z + 2 * n_dp
+    return first, second, jnp.where(late == 0, by_z, by_y)
+
+
 def fused(
     sizes,
-    picked_ref,
-    slot_ref,
     len_ref,
+    state_table_ref,
+    page_table_ref,
     states_ref,
     pages_ref,
     q_ref,
@@ -89,6 +133,21 @@
     recall_ref,
     mla_ref,
     records,
+    q_buf,
+    k_buf,
+    v_buf,
+    gate_buf,
+    beta_buf,
+    mq_buf,
+    new_buf,
+    wuk_buf,
+    wuv_buf,
+    state_slots,
+    page_slots,
+    picked_rows,
+    place_row,
+    picked,
+    place,
     outgoing,
     incoming,
     lift_out,
@@ -99,8 +158,9 @@
     result_out,
     coefs,
     offsets,
-    x_send_sem,
-    x_recv_sem,
+    send_sem,
+    first_sem,
+    second_sem,
     swap_send_sem,
     swap_recv_sem,
     lift_send_sem,
@@ -109,68 +169,175 @@
     wuv_recv_sem,
     back_send_sem,
     back_recv_sem,
+    record_sem,
+    load_sem,
+    table_sem,
 ):
-    n_dp, n_t, cap = sizes
+    n_z, n_y, n_t = sizes
+    n_dp = n_z * n_y
+    side = (n_z, n_y)
     heads, slots, hd, _ = states_ref.shape
     page_len, latent = pages_ref.shape[2], pages_ref.shape[3]
     rows, tokens, _ = q_ref.shape
     folds = latent // hd
     me = lax.axis_index("dp")
     mine = lax.axis_index("tensor")
+    at_z, at_y = me // n_y, me % n_y
+
+    n_local = heads * slots
+    record_loads = [
+        pltpu.make_async_copy(
+            states_ref.at[h], records.at[pl.ds(h * slots, slots)], record_sem.at[h]
+        )
+        for h in range(heads)
+    ] + [
+        pltpu.make_async_copy(
+            pages_ref.at[0, :, :, f * hd : (f + 1) * hd],
+            records.at[pl.ds(n_local, pages_ref.shape[1]), f * page_len : (f + 1) * page_len, :],
+            record_sem.at[heads + f],
+        )
+        for f in range(folds)
+    ]
+    loads = [
+        pltpu.make_async_copy(source, target, load_sem.at[i])
+        for i, (source, target) in enumerate(
+            (
+                (mq_ref, mq_buf),
+                (wuk_ref, wuk_buf),
+                (wuv_ref, wuv_buf),
+                (q_ref, q_buf),
+                (k_ref, k_buf),
+                (v_ref, v_buf),
+                (gate_ref, gate_buf),
+                (beta_ref, beta_buf),
+                (new_ref, new_buf),
+            )
+        )
+    ]
+    table_loads = [
+        pltpu.make_async_copy(state_table_ref, state_slots, table_sem.at[0]),
+        pltpu.make_async_copy(page_table_ref.at[mine], page_slots, table_sem.at[1]),
+    ]
+    for load in table_loads + record_loads + loads:
+        load.start()
 
     barrier = pltpu.get_barrier_semaphore()
 
-    def greet_dp(k, c):
-        pl.semaphore_signal(barrier, inc=1, device_id={"dp": (me + k) % n_dp})
+    def greet_z(k, c):
+        pl.semaphore_signal(barrier, inc=1, device_id={"dp": ((at_z + k) % n_z) * n_y + at_y})
+        return c
+
+    def greet_y(k, c):
+        pl.semaphore_signal(barrier, inc=1, device_id={"dp": at_z * n_y + (at_y + k) % n_y})
         return c
 
     def greet_tensor(k, c):
         pl.semaphore_signal(barrier, inc=1, device_id={"tensor": (mine + k) % n_t})
         return c
 
-    lax.fori_loop(1, n_dp, greet_dp, 0)
+    lax.fori_loop(1, n_z, greet_z, 0)
+    lax.fori_loop(1, n_y, greet_y, 0)
     lax.fori_loop(1, n_t, greet_tensor, 0)
 
-    def put_state(i, c):
-        records[i] = states_ref[i // slots, i % slots]
-        return c
-
-    def put_page(i, c):
-        page = pages_ref[0, i]
-        for f in range(folds):
-            records[heads * slots + i, f * page_len : (f + 1) * page_len, :] = page[
-                :, f * hd : (f + 1) * hd
-            ]
-        return c
-
-    lax.fori_loop(0, heads * slots, put_state, 0)
-    lax.fori_loop(0, pages_ref.shape[1], put_page, 0)
-    for s in range(cap):
-        incoming[me * cap + s] = records[picked_ref[me * cap + s]]
-
-    pl.semaphore_wait(barrier, n_dp + n_t - 2)
-
-    def send_records(k, c):
-        peer = (me + (k * 27) % n_dp) % n_dp
-        for s in range(cap):
-            outgoing[peer * cap + s] = records[picked_ref[peer * cap + s]]
-        pltpu.make_async_remote_copy(
-            src_ref=outgoing.at[pl.ds(peer * cap, cap)],
-            dst_ref=incoming.at[pl.ds(me * cap, cap)],
-            send_sem=x_send_sem,
-            recv_sem=x_recv_sem,
-            device_id={"dp": peer},
-        ).start()
-        return c
-
-    lax.fori_loop(1, n_dp, send_records, 0)
+    for load in table_loads:
+        load.wait()
+    mine_slots = state_slots[0:heads, :]
+    for t in range(1, n_t):
+        mine_slots = jnp.where(mine == t, state_slots[t * heads : (t + 1) * heads, :], mine_slots)
+    first, second, slot = routes(
+        mine_slots,
+        page_slots[...],
+        me,
+        (n_z, n_y),
+        rows,
+        slots,
+        pages_ref.shape[1],
+    )
+    picked_rows[0:1, :] = first
+    picked_rows[1:2, :] = second
+    place_row[...] = slot
+    scalars = [
+        pltpu.make_async_copy(picked_rows, picked, table_sem.at[2]),
+        pltpu.make_async_copy(place_row, place, table_sem.at[3]),
+    ]
+    for load in scalars:
+        load.start()
+    for load in scalars + record_loads:
+        load.wait()
+
+    def hop(which, leg, k):
+        along_z = which == leg
+        if along_z:
+            return {"dp": ((at_z + k) % n_z) * n_y + at_y}
+        return {"dp": at_z * n_y + (at_y + k) % n_y}
+
+    def stage(which, k, j):
+        over_z, over_y = (k, j) if which == 0 else (j, k)
+        target = ((at_z + over_z) % n_z) * n_y + (at_y + over_y) % n_y
+        return records[picked[which, target * rows]]
+
+    def nearest(i, n):
+        return (((i + 1) // 2) * (1 - 2 * ((i + 1) % 2)) + n) % n
+
+    def spot(which, leg, k, j):
+        return ((2 * which + leg) * side[which] + k) * side[1 - which] + j
+
+    def first_leg(which, k):
+        return pltpu.make_async_remote_copy(
+            src_ref=outgoing.at[which, k],
+            dst_ref=incoming.at[pl.ds(spot(which, 0, k, 0), side[1 - which])],
+            send_sem=send_sem.at[which, 0, k],
+            recv_sem=first_sem.at[which, k],
+            device_id=hop(which, 0, k),
+        )
+
+    def second_leg(which, k, j, own):
+        held = outgoing.at[which, k, j] if own else incoming.at[spot(which, 0, k, j)]
+        return pltpu.make_async_remote_copy(
+            src_ref=held,
+            dst_ref=incoming.at[spot(which, 1, k, j)],
+            send_sem=send_sem.at[which, 1, j],
+            recv_sem=second_sem.at[which, j],
+            device_id=hop(which, 1, j),
+        )
+
+    def forward(which, k, own):
+        n = side[1 - which]
+
+        def one(i, c):
+            second_leg(which, k, nearest(i, n), own).start()
+            return c
+
+        lax.fori_loop(1, n, one, 0)
+
+    for which in range(2):
+        incoming[spot(which, 0, 0, 0)] = stage(which, 0, 0)
+
+    pl.semaphore_wait(barrier, n_z + n_y + n_t - 3)
+
+    def send_first(which, k):
+        for j in range(side[1 - which]):
+            outgoing[which, k, j] = stage(which, k, j)
+        first_leg(which, k).start()
+
+    for i in range(1, max(side)):
+        for which in range(2):
+            if i < side[which]:
+                send_first(which, nearest(i, side[which]))
+    for which in range(2):
+        for j in range(1, side[1 - which]):
+            outgoing[which, 0, j] = stage(which, 0, j)
+        forward(which, 0, True)
+
+    for load in loads:
+        load.wait()
 
     for h in range(heads):
-        queries = mq_ref[:, :, h * hd : (h + 1) * hd].reshape(rows * tokens, hd)
-        lifted = mm(queries, wuk_ref[h]).astype(BF16)
+        queries = mq_buf[:, :, h * hd : (h + 1) * hd].reshape(rows * tokens, hd)
+        lifted = mm(queries, wuk_buf[h]).astype(BF16)
         lift_out[:, h] = lifted.reshape(rows, tokens, latent)
     lift_in[0] = lift_out[mine]
-    wuv_in[0] = wuv_ref[...]
+    wuv_in[0] = wuv_buf[...]
 
     def lift_copy(k):
         peer = (mine + k) % n_t
@@ -185,7 +352,7 @@
     def wuv_copy(k):
         peer = (mine + k) % n_t
         return pltpu.make_async_remote_copy(
-            src_ref=wuv_ref,
+            src_ref=wuv_buf,
             dst_ref=wuv_in.at[n_t - k],
             send_sem=wuv_send_sem.at[k],
             recv_sem=wuv_recv_sem.at[n_t - k],
@@ -221,14 +388,14 @@
         alive = (
             lax.broadcasted_iota(jnp.int32, (heads * tokens, 1), 0) % tokens < len_ref[r]
         ).astype(F32)
-        raw = beta_ref[r].astype(F32)
+        raw = beta_buf[r].astype(F32)
         betas = jnp.concatenate([raw[:, h : h + 1] for h in range(heads)], axis=0)
         betas = alive / (1.0 + jnp.exp(-betas))
         coefficient, offset = recall_coefficients(
-            stack_heads(q_ref[r], heads, hd),
-            stack_heads(k_ref[r], heads, hd),
-            stack_heads(v_ref[r], heads, hd),
-            stack_heads(gate_ref[r], heads, hd),
+            stack_heads(q_buf[r], heads, hd),
+            stack_heads(k_buf[r], heads, hd),
+            stack_heads(v_buf[r], heads, hd),
+            stack_heads(gate_buf[r], heads, hd),
             betas,
             alive,
             tokens,
@@ -237,22 +404,37 @@
         offsets[r] = offset
         return c
 
-    lax.fori_loop(0, rows, make_coefficients, 0)
-
-    fresh = new_ref[mine]
+    def pass_on(i, c):
+        for which in range(2):
+            k = nearest(i, side[which])
+            first_leg(which, k).wait_recv()
+            forward(which, k, False)
+        return c
+
+    def work(i, c):
+        make_coefficients(i - 1, c)
+        return pass_on(i, c)
+
+    assert n_z == n_y
+    paired = min(rows, n_z - 1)
+    lax.fori_loop(1, paired + 1, work, 0)
+    lax.fori_loop(paired + 1, n_z, pass_on, 0)
+    lax.fori_loop(paired, rows, make_coefficients, 0)
+
+    fresh = new_buf[mine]
     context[n_t] = jnp.concatenate(
         [fresh, jnp.zeros((context.shape[1] - tokens, latent), BF16)], axis=0
     )
 
-    away = (n_dp - 1) * cap
-    pltpu.make_async_copy(
-        incoming.at[pl.ds(0, away)], incoming.at[pl.ds(0, away)], x_recv_sem
-    ).wait()
+    for which in range(2):
+        for j in range(1, side[1 - which]):
+            column = incoming.at[pl.ds(spot(which, 1, 0, 0), side[which])]
+            pltpu.make_async_copy(column, column, second_sem.at[which, j]).wait()
 
     n_states = heads * rows
 
     def place_page(i, c):
-        record = incoming[slot_ref[n_states + i]]
+        record = incoming[place[0, n_states + (i % pages_row) * rows + i // pages_row]]
         for f in range(folds):
             page_out[
                 i // pages_row,
@@ -270,7 +452,7 @@
     def recall(r, c):
         alive = (lax.broadcasted_iota(jnp.int32, (tokens, 1), 0) < len_ref[r]).astype(F32)
         for h in range(heads):
-            state = incoming[slot_ref[h * rows + r]]
+            state = incoming[place[0, h * rows + r]]
             high, low = halves(coefs[r, h * tokens : (h + 1) * tokens, :])
             both = mm(jnp.concatenate([high, low], axis=0), state)
             seen = both[:tokens] + both[tokens:] + offsets[r, h * tokens : (h + 1) * tokens, :]
@@ -323,18 +505,19 @@
         wuv_copy(k).wait_send()
         page_copy(k).wait_send()
         back_copy(k).wait_send()
-    pltpu.make_async_copy(
-        outgoing.at[pl.ds(0, away)], outgoing.at[pl.ds(0, away)], x_send_sem
-    ).wait()
+    for which in range(2):
+        for k in range(1, side[which]):
+            first_leg(which, k).wait_send()
+        for j in range(1, side[1 - which]):
+            column = incoming.at[pl.ds(spot(which, 1, 0, 0), side[which])]
+            pltpu.make_async_copy(column, column, send_sem.at[which, 1, j]).wait()
 
 
 def run_fused(
-    n_dp,
-    n_t,
-    cap,
-    picked,
-    slot,
+    sizes,
     tool_len,
+    state_table,
+    page_table,
     kda_pool,
     latent_pool,
     kda_q,
@@ -351,19 +534,37 @@
     _, pool_pages, page_len, latent = latent_pool.shape
     rows, tokens, _ = kda_q.shape
     pages_row = pool_pages // rows
+    n_z, n_y, n_t = sizes
+    n_dp = n_z * n_y
+    lanes = state_table.shape[1]
     vmem = pl.BlockSpec(memory_space=pltpu.VMEM)
     smem = pl.BlockSpec(memory_space=pltpu.SMEM)
     out = jax.ShapeDtypeStruct(kda_q.shape, BF16)
     dma = pltpu.SemaphoreType.DMA
     return pl.pallas_call(
-        functools.partial(fused, (n_dp, n_t, cap)),
+        functools.partial(fused, sizes),
         out_shape=(out, out),
-        in_specs=[smem] * 3 + [vmem] * 11,
+        in_specs=[smem] + [pl.BlockSpec(memory_space=pl.ANY)] * 13,
         out_specs=(vmem, vmem),
         scratch_shapes=[
             pltpu.VMEM((heads * slots + pool_pages, hd, hd), BF16),
-            pltpu.VMEM((n_dp * cap, hd, hd), BF16),
-            pltpu.VMEM((n_dp * cap, hd, hd), BF16),
+            pltpu.VMEM(kda_q.shape, BF16),
+            pltpu.VMEM(kda_k.shape, BF16),
+            pltpu.VMEM(kda_v.shape, BF16),
+            pltpu.VMEM(kda_gate.shape, BF16),
+            pltpu.VMEM(kda_beta.shape, BF16),
+            pltpu.VMEM(mla_q.shape, BF16),
+            pltpu.VMEM(mla_new.shape, BF16),
+            pltpu.VMEM(w_uk.shape, BF16),
+            pltpu.VMEM(w_uv.shape, BF16),
+            pltpu.VMEM(state_table.shape, jnp.int32),
+            pltpu.VMEM(page_table.shape[1:], jnp.int32),
+            pltpu.VMEM((2, lanes), jnp.int32),
+            pltpu.VMEM((1, LANES), jnp.int32),
+            pltpu.SMEM((2, lanes), jnp.int32),
+            pltpu.SMEM((1, LANES), jnp.int32),
+            pltpu.VMEM((2, n_z, n_y, hd, hd), BF16),
+            pltpu.VMEM((4 * n_dp, hd, hd), BF16),
             pltpu.VMEM((rows, heads, tokens, latent), BF16),
             pltpu.VMEM((n_t, heads, tokens, latent), BF16),
             pltpu.VMEM((n_t, heads, latent, hd), BF16),
@@ -372,17 +573,19 @@
             pltpu.VMEM((n_t, tokens, heads * hd), BF16),
             pltpu.VMEM((rows, heads * tokens, hd), F32),
             pltpu.VMEM((rows, heads * tokens, hd), F32),
-            dma,
-            dma,
+            dma((2, 2, max(n_z, n_y))),
+            dma((2, max(n_z, n_y))),
+            dma((2, max(n_z, n_y))),
         ]
-        + [dma((n_t,))] * 8,
+        + [dma((n_t,))] * 8
+        + [dma((heads + latent // hd,)), dma((9,)), dma((4,))],
         compiler_params=pltpu.CompilerParams(
-            collective_id=0, has_side_effects=True, vmem_limit_bytes=48 * 1024 * 1024
+            collective_id=0, has_side_effects=True, vmem_limit_bytes=60 * 1024 * 1024
         ),
     )(
-        picked,
-        slot,
         tool_len,
+        state_table,
+        page_table,
         kda_pool,
         latent_pool,
         kda_q,
@@ -395,31 +598,6 @@
         w_uk,
         w_uv,
     )
-
-
-def routes(state_table, page_table, n_dp, heads, rows, pool_pages):
-    me = lax.axis_index("dp")
-    mine = lax.axis_index("tensor")
-    pages_row = page_table.shape[2]
-    states = lax.dynamic_slice_in_dim(state_table, mine * heads, heads, 1).T
-    pages = lax.dynamic_index_in_dim(page_table, mine, 1, keepdims=False).T
-    owners = jnp.concatenate([states // rows, pages // pool_pages], axis=0)
-    head = lax.broadcasted_iota(jnp.int32, states.shape, 0)
-    ids = jnp.concatenate([head * rows + states % rows, heads * rows + pages % pool_pages], axis=0)
-    kinds = heads + pages_row
-    here = (owners == me).reshape(kinds, n_dp, rows)
-    ids3 = ids.reshape(kinds, n_dp, rows)
-    top = heads * rows + pool_pages - 1
-    first = jnp.min(jnp.where(here, ids3, top), axis=(0, 2))
-    second = jnp.max(jnp.where(here, ids3, 0), axis=(0, 2))
-    picked = jnp.stack([first, second], axis=1).reshape(-1)
-    own = lax.dynamic_slice_in_dim(owners, me * rows, rows, 1)
-    own_ids = lax.dynamic_slice_in_dim(ids, me * rows, rows, 1)
-    own = jnp.concatenate([own[:heads].reshape(-1), own[heads:].T.reshape(-1)])
-    own_ids = jnp.concatenate([own_ids[:heads].reshape(-1), own_ids[heads:].T.reshape(-1)])
-    behind = (own[None, :] == own[:, None]) & (own_ids[None, :] < own_ids[:, None])
-    slot = 2 * own + jnp.any(behind, axis=1).astype(jnp.int32)
-    return picked, slot
 
 
 def local(
@@ -439,16 +617,11 @@
     w_uv,
 ):
     n_dp, n_t = lax.axis_size("dp"), lax.axis_size("tensor")
-    picked, slot = routes(
-        state_table, page_table, n_dp, kda_pool.shape[0], tool_len.shape[0], latent_pool.shape[1]
-    )
     return run_fused(
-        n_dp,
-        n_t,
-        2,
-        picked,
-        slot,
+        (n_dp // SIDE_Y, SIDE_Y, n_t),
         tool_len,
+        state_table.T,
+        jnp.transpose(page_table, (1, 2, 0)),
         kda_pool,
         latent_pool,
         kda_q,

time: 186 us -> 136 us (0.73)
  the two profiles are of different devices: /device:TPU:27 before, /device:TPU:1 now
where the time goes in v2:
time: 136 us
  Pallas kernels  132 us (97%)
  local copies, waits for them, and re-layouts  3.88 us (3%)
    pallas_call x1, Pallas kernels, run_fused(): pl.pallas_call(functools.partial(fused, sizes), out_shape=(out, out), in_...  132 us
    unnamed x5, local copies, waits for them, and re-layouts  3.88 us

profile of v2, /device:TPU:1, one launch (start us, length us, event | category | flops | bytes accessed | tf_op | source)
XLA Modules:
  0.0 136.2 jit_solution(8516342946084148587)
XLA Ops:
  0.6 1.5 %copy.16.beta_ref = bf16[8,32,4]{2,1,0:T(8,128)(2,1)} copy(bf16[8,32,4]{1,2,0:T(4,128)(2,1)} %param.23) | data formatting | bytes 4096 | tf_op args[9]
  2.1 131.7 %shard_map.149 = (bf16[8,32,512]{2,1,0:T(8,128)(2,1)}, bf16[8,32,512]{2,1,0:T(8,128)(2,1)}) custom-call(s32[8]{0:T(128)} %len_ref.1, s32[32,512]{1,0:T(8,128)} %bitcast.2, s32[8,4,512]{2,1,0:T(4,128)} %bitcast.3, bf16[4,8,128,128]{3,2,1,0:T(8,128)(2,1)} %states_ref.1, bf16[1,32,32,512]{3,2,1,0:T(8,128)(2,1)} %pages_ref.1, bf16[8,32,512]{2,1,0:T(8,128)(2,1)} %q_ref.1, ...), custom_call_target="tpu_custom_call" | custom-call | tf_op jit(solution)/shard_map/pallas_call | solution.py:544
  133.8 0.0 copy-start
  133.8 1.7 %copy.19 = bf16[8,32,512]{2,1,0:T(8,128)(2,1)} copy(bf16[8,32,512]{2,1,0:T(8,128)(2,1)} %get-tuple-element.4) | data formatting | bytes 524288
  135.5 0.0 copy-done
  135.5 0.7 copy.20
Async XLA Ops:
  133.8 1.7 %copy-start = (bf16[8,32,512]{2,1,0:T(8,128)(2,1)S(1)}, bf16[8,32,512]{2,1,0:T(8,128)(2,1)}, u32[]{:S(2)}) copy-start(bf16[8,32,512]{2,1,0:T(8,128)(2,1)} %get-tuple-element.5) | copy-start | bytes 786436

commit v3 on v2

--- a/solution.py
+++ b/solution.py
@@ -130,8 +130,7 @@
     new_ref,
     wuk_ref,
     wuv_ref,
-    recall_ref,
-    mla_ref,
+    out_ref,
     records,
     q_buf,
     k_buf,
@@ -158,6 +157,7 @@
     result_out,
     coefs,
     offsets,
+    scores,
     send_sem,
     first_sem,
     second_sem,
@@ -176,6 +176,7 @@
     n_z, n_y, n_t = sizes
     n_dp = n_z * n_y
     side = (n_z, n_y)
+    recall_ref, mla_ref = out_ref.at[0], out_ref.at[1]
     heads, slots, hd, _ = states_ref.shape
     page_len, latent = pages_ref.shape[2], pages_ref.shape[3]
     rows, tokens, _ = q_ref.shape
@@ -389,8 +390,13 @@
             lax.broadcasted_iota(jnp.int32, (heads * tokens, 1), 0) % tokens < len_ref[r]
         ).astype(F32)
         raw = beta_buf[r].astype(F32)
-        betas = jnp.concatenate([raw[:, h : h + 1] for h in range(heads)], axis=0)
-        betas = alive / (1.0 + jnp.exp(-betas))
+        raw = jnp.concatenate([raw[h : h + 1] for h in range(heads)], axis=1)
+        square = (heads * tokens, heads * tokens)
+        diagonal = lax.broadcasted_iota(jnp.int32, square, 0) == lax.broadcasted_iota(
+            jnp.int32, square, 1
+        )
+        raw = jnp.sum(jnp.where(diagonal, raw, 0.0), axis=1, keepdims=True)
+        betas = alive / (1.0 + jnp.exp(-raw))
         coefficient, offset = recall_coefficients(
             stack_heads(q_buf[r], heads, hd),
             stack_heads(k_buf[r], heads, hd),
@@ -446,8 +452,8 @@
     pages_row = page_out.shape[1] // page_len
     lax.fori_loop(0, rows * pages_row, place_page, 0)
     context[0] = page_out[mine]
-    for k in range(1, n_t):
-        page_copy(k).start()
+    for i in range(n_t - 1, 0, -1):
+        page_copy(nearest(i, n_t)).start()
 
     def recall(r, c):
         alive = (lax.broadcasted_iota(jnp.int32, (tokens, 1), 0) < len_ref[r]).astype(F32)
@@ -464,38 +470,58 @@
     for k in range(1, n_t):
         lift_copy(k).wait_recv()
         wuv_copy(k).wait_recv()
-    for k in range(1, n_t):
-        page_copy(k).wait_recv()
 
     every = heads * tokens
+    queries = n_t * every
+    width = context.shape[1]
+
+    def score(i):
+        scores[i] = mm_nt(lift_in[...].reshape(queries, latent), context[i])
+
+    def score_arrived(i, c):
+        k = nearest(i, n_t)
+        page_copy(n_t - k).wait_recv()
+        score(k)
+        return c
+
+    score(n_t)
+    score(0)
+    lax.fori_loop(1, n_t, score_arrived, 0)
+
+    group = 2
     scale = hd ** (-0.5)
-    total_keys = context.shape[0] * context.shape[1]
-    old_keys = n_t * context.shape[1]
-    column = lax.broadcasted_iota(jnp.int32, (every, total_keys), 1) - old_keys
-    token = lax.broadcasted_iota(jnp.int32, (every, total_keys), 0) % tokens
+    seen_shape = (group * every, width)
+    column = lax.broadcasted_iota(jnp.int32, seen_shape, 1)
+    token = lax.broadcasted_iota(jnp.int32, seen_shape, 0) % tokens
     row_alive = (lax.broadcasted_iota(jnp.int32, (tokens, 1), 0) < len_ref[mine]).astype(F32)
 
-    def attend(k):
-        keys = context[...].reshape(total_keys, latent)
-        queries = lift_in[k].reshape(every, latent)
-        scores = mm_nt(queries, keys) * scale
-        scores = jnp.where(column <= token, scores, -1e30)
-        top = jnp.max(scores, axis=-1, keepdims=True)
-        e = jnp.exp(scores - top)
-        total = jnp.sum(e, axis=-1, keepdims=True)
-        mixed = mm(e.astype(BF16), keys)
+    def attend(i):
+        start = pl.multiple_of(i * group * every, group * every)
+        parts = [scores[c, pl.ds(start, group * every), :] * scale for c in range(n_t + 1)]
+        parts[n_t] = jnp.where(column <= token, parts[n_t], -1e30)
+        top = functools.reduce(jnp.maximum, parts)
+        top = jnp.max(top, axis=-1, keepdims=True)
+        parts = [jnp.exp(part - top) for part in parts]
+        total = jnp.sum(functools.reduce(jnp.add, parts), axis=-1, keepdims=True)
+        weights = jnp.concatenate([part.astype(BF16) for part in parts], axis=1)
+        mixed = mm(weights, context[...].reshape((n_t + 1) * width, latent))
         attended = (mixed / total).astype(BF16)
-        for h in range(heads):
-            out = mm(attended[h * tokens : (h + 1) * tokens], wuv_in[k, h]) * row_alive
-            result_out[k, :, h * hd : (h + 1) * hd] = out.astype(BF16)
-
-    def attend_away(k, c):
-        attend(k)
-        back_copy(k).start()
-        return c
-
-    lax.fori_loop(1, n_t, attend_away, 0)
+        for g in range(group):
+            for h in range(heads):
+                first = (g * heads + h) * tokens
+                out = mm(attended[first : first + tokens], wuv_in[i * group + g, h]) * row_alive
+                result_out[i * group + g, :, h * hd : (h + 1) * hd] = out.astype(BF16)
+
+    def attend_away(i, c):
+        attend(i)
+        for g in range(group):
+            back_copy(i * group + g).start()
+        return c
+
+    lax.fori_loop(1, n_t // group, attend_away, 0)
     attend(0)
+    for g in range(1, group):
+        back_copy(g).start()
     mla_ref[mine] = result_out[0]
 
     for k in range(1, n_t):
@@ -539,13 +565,13 @@
     lanes = state_table.shape[1]
     vmem = pl.BlockSpec(memory_space=pltpu.VMEM)
     smem = pl.BlockSpec(memory_space=pltpu.SMEM)
-    out = jax.ShapeDtypeStruct(kda_q.shape, BF16)
+    out = jax.ShapeDtypeStruct((2,) + kda_q.shape, BF16)
     dma = pltpu.SemaphoreType.DMA
-    return pl.pallas_call(
+    both = pl.pallas_call(
         functools.partial(fused, sizes),
-        out_shape=(out, out),
+        out_shape=out,
         in_specs=[smem] + [pl.BlockSpec(memory_space=pl.ANY)] * 13,
-        out_specs=(vmem, vmem),
+        out_specs=vmem,
         scratch_shapes=[
             pltpu.VMEM((heads * slots + pool_pages, hd, hd), BF16),
             pltpu.VMEM(kda_q.shape, BF16),
@@ -573,6 +599,7 @@
             pltpu.VMEM((n_t, tokens, heads * hd), BF16),
             pltpu.VMEM((rows, heads * tokens, hd), F32),
             pltpu.VMEM((rows, heads * tokens, hd), F32),
+            pltpu.VMEM((n_t + 1, n_t * heads * tokens, pages_row * page_len), F32),
             dma((2, 2, max(n_z, n_y))),
             dma((2, max(n_z, n_y))),
             dma((2, max(n_z, n_y))),
@@ -598,6 +625,7 @@
         w_uk,
         w_uv,
     )
+    return both[0], both[1]
 
 
 def local(
@@ -628,7 +656,7 @@
         kda_k,
         kda_v,
         kda_gate,
-        kda_beta,
+        jnp.transpose(kda_beta, (0, 2, 1)),
         mla_q,
         mla_new,
         w_uk,

time: 136 us -> 133 us (0.978)
  local copies, waits for them, and re-layouts: 3.88 us -> 1.87 us
  Pallas kernels: 132 us -> 130 us
    unnamed x5 -> x0, local copies, waits for them, and re-layouts: 3.88 us -> none
    squeeze x0 -> x1, local copies, waits for them, and re-layouts: none -> 1.87 us  [run_fused(): return (both[0], both[1])]
    pallas_call x1, Pallas kernels: 132 us -> 130 us  [run_fused(): pl.pallas_call(functools.partial(fused, sizes), out_shape=out, in_specs=[...]
where the time goes in v3:
time: 133 us; the launch traced here: 132 us
  Pallas kernels  130 us (98%)
  local copies, waits for them, and re-layouts  1.87 us (1%)
    pallas_call x1, Pallas kernels, run_fused(): pl.pallas_call(functools.partial(fused, sizes), out_shape=out, in_specs=[...  130 us

profile of v3, /device:TPU:1, one launch (start us, length us, event | category | flops | bytes accessed | tf_op | source)
XLA Modules:
  0.0 132.5 jit_solution(5886468148000026009)
XLA Ops:
  0.6 130.0 %shard_map.149 = bf16[2,8,32,512]{3,2,1,0:T(8,128)(2,1)} custom-call(s32[8]{0:T(128)} %len_ref.1, s32[32,512]{1,0:T(8,128)} %bitcast.7, s32[8,4,512]{2,1,0:T(4,128)} %bitcast.8, bf16[4,8,128,128]{3,2,1,0:T(8,128)(2,1)} %states_ref.1, bf16[1,32,32,512]{3,2,1,0:T(8,128)(2,1)} %pages_ref.1, bf16[8,32,512]{2,1,0:T(8,128)(2,1)} %q_ref.1, ...), custom_call_target="tpu_custom_call" | custom-call | tf_op jit(solution)/shard_map/pallas_call | solution.py:570
  130.6 1.9 %slice_bitcast_fusion = (bf16[8,32,512]{2,1,0:T(8,128)(2,1)}, bf16[8,32,512]{2,1,0:T(8,128)(2,1)}) fusion(bf16[2,8,32,512]{3,2,1,0:T(8,128)(2,1)} %shard_map.149), kind=kLoop, calls=%fused_computation | loop fusion | bytes 1048576 | tf_op jit(solution)/shard_map/squeeze | solution.py:628

commit v4 on v3

--- a/solution.py
+++ b/solution.py
@@ -157,7 +157,9 @@
     result_out,
     coefs,
     offsets,
-    scores,
+    tops,
+    sums,
+    mixes,
     send_sem,
     first_sem,
     second_sem,
@@ -452,8 +454,18 @@
     pages_row = page_out.shape[1] // page_len
     lax.fori_loop(0, rows * pages_row, place_page, 0)
     context[0] = page_out[mine]
-    for i in range(n_t - 1, 0, -1):
-        page_copy(nearest(i, n_t)).start()
+    odd = mine % 2
+    twin = 1 + (n_t - 2) * odd
+    far = n_t // 4
+    near_chips = [p for p in range(1, n_t // 2) if p != far]
+
+    def cores(p):
+        return (2 * p - odd, 2 * p + 1 - odd)
+
+    page_copy(twin).start()
+    for p in near_chips + [far]:
+        for k in cores(p):
+            page_copy(k).start()
 
     def recall(r, c):
         alive = (lax.broadcasted_iota(jnp.int32, (tokens, 1), 0) < len_ref[r]).astype(F32)
@@ -472,56 +484,63 @@
         wuv_copy(k).wait_recv()
 
     every = heads * tokens
-    queries = n_t * every
     width = context.shape[1]
-
-    def score(i):
-        scores[i] = mm_nt(lift_in[...].reshape(queries, latent), context[i])
-
-    def score_arrived(i, c):
-        k = nearest(i, n_t)
+    group = 2
+    size = group * every
+    scale = hd ** (-0.5)
+    column = lax.broadcasted_iota(jnp.int32, (size, width), 1)
+    token = lax.broadcasted_iota(jnp.int32, (size, width), 0) % tokens
+    row_alive = (lax.broadcasted_iota(jnp.int32, (tokens, 1), 0) < len_ref[mine]).astype(F32)
+
+    def asked(i):
+        return lift_in[i * group : (i + 1) * group].reshape(size, latent)
+
+    def chip(p):
+        return context[pl.ds(2 * p - odd, 2)].reshape(2 * width, latent)
+
+    def arrive(k):
         page_copy(n_t - k).wait_recv()
-        score(k)
-        return c
-
-    score(n_t)
-    score(0)
-    lax.fori_loop(1, n_t, score_arrived, 0)
-
-    group = 2
-    scale = hd ** (-0.5)
-    seen_shape = (group * every, width)
-    column = lax.broadcasted_iota(jnp.int32, seen_shape, 1)
-    token = lax.broadcasted_iota(jnp.int32, seen_shape, 0) % tokens
-    row_alive = (lax.broadcasted_iota(jnp.int32, (tokens, 1), 0) < len_ref[mine]).astype(F32)
-
-    def attend(i):
-        start = pl.multiple_of(i * group * every, group * every)
-        parts = [scores[c, pl.ds(start, group * every), :] * scale for c in range(n_t + 1)]
-        parts[n_t] = jnp.where(column <= token, parts[n_t], -1e30)
-        top = functools.reduce(jnp.maximum, parts)
-        top = jnp.max(top, axis=-1, keepdims=True)
+
+    arrive(twin)
+    for p in near_chips:
+        for k in cores(p):
+            arrive(k)
+    for i in range(n_t // group):
+        span = slice(i * size, (i + 1) * size)
+        keys = [context[n_t], context[0], context[twin]] + [chip(p) for p in near_chips]
+        parts = [mm_nt(asked(i), key) * scale for key in keys]
+        parts[0] = jnp.where(column <= token, parts[0], -1e30)
+        top = functools.reduce(
+            jnp.maximum, [jnp.max(part, axis=-1, keepdims=True) for part in parts]
+        )
         parts = [jnp.exp(part - top) for part in parts]
-        total = jnp.sum(functools.reduce(jnp.add, parts), axis=-1, keepdims=True)
-        weights = jnp.concatenate([part.astype(BF16) for part in parts], axis=1)
-        mixed = mm(weights, context[...].reshape((n_t + 1) * width, latent))
-        attended = (mixed / total).astype(BF16)
+        tops[span] = top
+        sums[span] = functools.reduce(
+            jnp.add, [jnp.sum(part, axis=-1, keepdims=True) for part in parts]
+        )
+        mixes[span] = functools.reduce(
+            jnp.add, [mm(part.astype(BF16), key) for part, key in zip(parts, keys)]
+        )
+
+    for k in cores(far):
+        arrive(k)
+    for i in [*range(1, n_t // group), 0]:
+        span = slice(i * size, (i + 1) * size)
+        key = chip(far)
+        part = mm_nt(asked(i), key) * scale
+        top = jnp.maximum(tops[span], jnp.max(part, axis=-1, keepdims=True))
+        part = jnp.exp(part - top)
+        fade = jnp.exp(tops[span] - top)
+        share = 1.0 / (fade * sums[span] + jnp.sum(part, axis=-1, keepdims=True))
+        attended = (fade * share * mixes[span] + share * mm(part.astype(BF16), key)).astype(BF16)
         for g in range(group):
+            k = i * group + g
             for h in range(heads):
                 first = (g * heads + h) * tokens
-                out = mm(attended[first : first + tokens], wuv_in[i * group + g, h]) * row_alive
-                result_out[i * group + g, :, h * hd : (h + 1) * hd] = out.astype(BF16)
-
-    def attend_away(i, c):
-        attend(i)
-        for g in range(group):
-            back_copy(i * group + g).start()
-        return c
-
-    lax.fori_loop(1, n_t // group, attend_away, 0)
-    attend(0)
-    for g in range(1, group):
-        back_copy(g).start()
+                out = mm(attended[first : first + tokens], wuv_in[k, h]) * row_alive
+                result_out[k, :, h * hd : (h + 1) * hd] = out.astype(BF16)
+            if k:
+                back_copy(k).start()
     mla_ref[mine] = result_out[0]
 
     for k in range(1, n_t):
@@ -599,7 +618,9 @@
             pltpu.VMEM((n_t, tokens, heads * hd), BF16),
             pltpu.VMEM((rows, heads * tokens, hd), F32),
             pltpu.VMEM((rows, heads * tokens, hd), F32),
-            pltpu.VMEM((n_t + 1, n_t * heads * tokens, pages_row * page_len), F32),
+            pltpu.VMEM((n_t * heads * tokens, 1), F32),
+            pltpu.VMEM((n_t * heads * tokens, 1), F32),
+            pltpu.VMEM((n_t * heads * tokens, latent), F32),
             dma((2, 2, max(n_z, n_y))),
             dma((2, max(n_z, n_y))),
             dma((2, max(n_z, n_y))),

time: 133 us -> 133 us (level)
  no operation moved by 1% of the time
where the time goes in v4:
time: 133 us; the launch traced here: 131 us
  Pallas kernels  129 us (97%)
  local copies, waits for them, and re-layouts  1.87 us (1%)
    pallas_call x1, Pallas kernels, run_fused(): pl.pallas_call(functools.partial(fused, sizes), out_shape=out, in_specs=[...  129 us

profile of v4, /device:TPU:1, one launch (start us, length us, event | category | flops | bytes accessed | tf_op | source)
XLA Modules:
  0.0 131.2 jit_solution(5721503185884877518)
XLA Ops:
  0.6 128.7 %shard_map.149 = bf16[2,8,32,512]{3,2,1,0:T(8,128)(2,1)} custom-call(s32[8]{0:T(128)} %len_ref.1, s32[32,512]{1,0:T(8,128)} %bitcast.7, s32[8,4,512]{2,1,0:T(4,128)} %bitcast.8, bf16[4,8,128,128]{3,2,1,0:T(8,128)(2,1)} %states_ref.1, bf16[1,32,32,512]{3,2,1,0:T(8,128)(2,1)} %pages_ref.1, bf16[8,32,512]{2,1,0:T(8,128)(2,1)} %q_ref.1, ...), custom_call_target="tpu_custom_call" | custom-call | tf_op jit(solution)/shard_map/pallas_call | solution.py:589
  129.4 1.9 %slice_bitcast_fusion = (bf16[8,32,512]{2,1,0:T(8,128)(2,1)}, bf16[8,32,512]{2,1,0:T(8,128)(2,1)}) fusion(bf16[2,8,32,512]{3,2,1,0:T(8,128)(2,1)} %shard_map.149), kind=kLoop, calls=%fused_computation | loop fusion | bytes 1048576 | tf_op jit(solution)/shard_map/squeeze | solution.py:649

commit v5 on v4

--- a/solution.py
+++ b/solution.py
@@ -218,7 +218,11 @@
         )
     ]
     table_loads = [
-        pltpu.make_async_copy(state_table_ref, state_slots, table_sem.at[0]),
+        pltpu.make_async_copy(
+            state_table_ref.at[pl.ds(pl.multiple_of(mine // 2 * (2 * heads), 2 * heads), 2 * heads)],
+            state_slots,
+            table_sem.at[0],
+        ),
         pltpu.make_async_copy(page_table_ref.at[mine], page_slots, table_sem.at[1]),
     ]
     for load in table_loads + record_loads + loads:
@@ -244,9 +248,7 @@
 
     for load in table_loads:
         load.wait()
-    mine_slots = state_slots[0:heads, :]
-    for t in range(1, n_t):
-        mine_slots = jnp.where(mine == t, state_slots[t * heads : (t + 1) * heads, :], mine_slots)
+    mine_slots = jnp.where(mine % 2 == 0, state_slots[0:heads, :], state_slots[heads : 2 * heads, :])
     first, second, slot = routes(
         mine_slots,
         page_slots[...],
@@ -323,14 +325,14 @@
             outgoing[which, k, j] = stage(which, k, j)
         first_leg(which, k).start()
 
+    for which in range(2):
+        for j in range(1, side[1 - which]):
+            outgoing[which, 0, j] = stage(which, 0, j)
+        forward(which, 0, True)
     for i in range(1, max(side)):
         for which in range(2):
             if i < side[which]:
                 send_first(which, nearest(i, side[which]))
-    for which in range(2):
-        for j in range(1, side[1 - which]):
-            outgoing[which, 0, j] = stage(which, 0, j)
-        forward(which, 0, True)
 
     for load in loads:
         load.wait()
@@ -501,38 +503,50 @@
     def arrive(k):
         page_copy(n_t - k).wait_recv()
 
+    def fold(i, keys, masked=False, opened=True):
+        span = slice(i * size, (i + 1) * size)
+        parts = [mm_nt(asked(i), key) * scale for key in keys]
+        if masked:
+            parts[0] = jnp.where(column <= token, parts[0], -1e30)
+        top = functools.reduce(
+            jnp.maximum,
+            [jnp.max(part, axis=-1, keepdims=True) for part in parts]
+            + ([tops[span]] if opened else []),
+        )
+        parts = [jnp.exp(part - top) for part in parts]
+        total = functools.reduce(
+            jnp.add, [jnp.sum(part, axis=-1, keepdims=True) for part in parts]
+        )
+        mixed = functools.reduce(
+            jnp.add, [mm(part.astype(BF16), key) for part, key in zip(parts, keys)]
+        )
+        if opened:
+            fade = jnp.exp(tops[span] - top)
+            total = total + fade * sums[span]
+            mixed = mixed + fade * mixes[span]
+        return span, top, total, mixed
+
+    def keep(span, top, total, mixed):
+        tops[span] = top
+        sums[span] = total
+        mixes[span] = mixed
+
+    groups = n_t // group
     arrive(twin)
+    for i in range(groups):
+        keep(*fold(i, [context[n_t], context[0], context[twin]], masked=True, opened=False))
     for p in near_chips:
         for k in cores(p):
             arrive(k)
-    for i in range(n_t // group):
-        span = slice(i * size, (i + 1) * size)
-        keys = [context[n_t], context[0], context[twin]] + [chip(p) for p in near_chips]
-        parts = [mm_nt(asked(i), key) * scale for key in keys]
-        parts[0] = jnp.where(column <= token, parts[0], -1e30)
-        top = functools.reduce(
-            jnp.maximum, [jnp.max(part, axis=-1, keepdims=True) for part in parts]
-        )
-        parts = [jnp.exp(part - top) for part in parts]
-        tops[span] = top
-        sums[span] = functools.reduce(
-            jnp.add, [jnp.sum(part, axis=-1, keepdims=True) for part in parts]
-        )
-        mixes[span] = functools.reduce(
-            jnp.add, [mm(part.astype(BF16), key) for part, key in zip(parts, keys)]
-        )
+    if near_chips:
+        for i in range(groups):
+            keep(*fold(i, [chip(p) for p in near_chips]))
 
     for k in cores(far):
         arrive(k)
-    for i in [*range(1, n_t // group), 0]:
-        span = slice(i * size, (i + 1) * size)
-        key = chip(far)
-        part = mm_nt(asked(i), key) * scale
-        top = jnp.maximum(tops[span], jnp.max(part, axis=-1, keepdims=True))
-        part = jnp.exp(part - top)
-        fade = jnp.exp(tops[span] - top)
-        share = 1.0 / (fade * sums[span] + jnp.sum(part, axis=-1, keepdims=True))
-        attended = (fade * share * mixes[span] + share * mm(part.astype(BF16), key)).astype(BF16)
+    for i in [*range(1, groups), 0]:
+        _, _, total, mixed = fold(i, [chip(far)])
+        attended = (mixed * (1.0 / total)).astype(BF16)
         for g in range(group):
             k = i * group + g
             for h in range(heads):
@@ -584,7 +598,7 @@
     lanes = state_table.shape[1]
     vmem = pl.BlockSpec(memory_space=pltpu.VMEM)
     smem = pl.BlockSpec(memory_space=pltpu.SMEM)
-    out = jax.ShapeDtypeStruct((2,) + kda_q.shape, BF16)
+    out = pltpu.VMEM((2,) + kda_q.shape, BF16)
     dma = pltpu.SemaphoreType.DMA
     both = pl.pallas_call(
         functools.partial(fused, sizes),
@@ -602,7 +616,7 @@
             pltpu.VMEM(mla_new.shape, BF16),
             pltpu.VMEM(w_uk.shape, BF16),
             pltpu.VMEM(w_uv.shape, BF16),
-            pltpu.VMEM(state_table.shape, jnp.int32),
+            pltpu.VMEM((2 * heads, lanes), jnp.int32),
             pltpu.VMEM(page_table.shape[1:], jnp.int32),
             pltpu.VMEM((2, lanes), jnp.int32),
             pltpu.VMEM((1, LANES), jnp.int32),

time: 133 us -> 130 us (0.977); the launches traced: 131 us -> 130 us
  no operation moved by 1% of the time
where the time goes in v5:
time: 130 us
  Pallas kernels  129 us (99%)
    pallas_call x1, Pallas kernels, run_fused(): pl.pallas_call(functools.partial(fused, sizes), out_shape=out, in_specs=[...  129 us

profile of v5, /device:TPU:1, one launch (start us, length us, event | category | flops | bytes accessed | tf_op | source)
XLA Modules:
  0.0 130.1 jit_solution(12594354141393936634)
XLA Ops:
  0.6 128.7 %shard_map.149 = bf16[2,8,32,512]{3,2,1,0:T(8,128)(2,1)S(1)} custom-call(s32[8]{0:T(128)} %len_ref.1, s32[32,512]{1,0:T(8,128)} %bitcast.7, s32[8,4,512]{2,1,0:T(4,128)} %bitcast.8, bf16[4,8,128,128]{3,2,1,0:T(8,128)(2,1)} %states_ref.1, bf16[1,32,32,512]{3,2,1,0:T(8,128)(2,1)} %pages_ref.1, bf16[8,32,512]{2,1,0:T(8,128)(2,1)} %q_ref.1, ...), custom_call_target="tpu_custom_call" | custom-call | tf_op jit(solution)/shard_map/pallas_call | solution.py:603
  129.3 0.8 slice_bitcast_fusion

commit v6 on v5

--- a/solution.py
+++ b/solution.py
@@ -207,7 +207,6 @@
             (
                 (mq_ref, mq_buf),
                 (wuk_ref, wuk_buf),
-                (wuv_ref, wuv_buf),
                 (q_ref, q_buf),
                 (k_ref, k_buf),
                 (v_ref, v_buf),
@@ -225,7 +224,13 @@
         ),
         pltpu.make_async_copy(page_table_ref.at[mine], page_slots, table_sem.at[1]),
     ]
-    for load in table_loads + record_loads + loads:
+    loads += [
+        pltpu.make_async_copy(
+            wuv_ref.at[h], wuv_buf.at[:, h * hd : (h + 1) * hd], load_sem.at[len(loads) + h]
+        )
+        for h in range(heads)
+    ]
+    for load in table_loads + record_loads:
         load.start()
 
     barrier = pltpu.get_barrier_semaphore()
@@ -245,6 +250,8 @@
     lax.fori_loop(1, n_z, greet_z, 0)
     lax.fori_loop(1, n_y, greet_y, 0)
     lax.fori_loop(1, n_t, greet_tensor, 0)
+    for load in loads:
+        load.start()
 
     for load in table_loads:
         load.wait()
@@ -544,15 +551,15 @@
 
     for k in cores(far):
         arrive(k)
-    for i in [*range(1, groups), 0]:
+    for i in [*range(groups // 2, groups), *range(1, groups // 2), 0]:
         _, _, total, mixed = fold(i, [chip(far)])
         attended = (mixed * (1.0 / total)).astype(BF16)
         for g in range(group):
             k = i * group + g
+            out = mm(attended[g * every : (g + 1) * every], wuv_in[k])
             for h in range(heads):
-                first = (g * heads + h) * tokens
-                out = mm(attended[first : first + tokens], wuv_in[k, h]) * row_alive
-                result_out[k, :, h * hd : (h + 1) * hd] = out.astype(BF16)
+                own = out[h * tokens : (h + 1) * tokens, h * hd : (h + 1) * hd] * row_alive
+                result_out[k, :, h * hd : (h + 1) * hd] = own.astype(BF16)
             if k:
                 back_copy(k).start()
     mla_ref[mine] = result_out[0]
@@ -615,7 +622,7 @@
             pltpu.VMEM(mla_q.shape, BF16),
             pltpu.VMEM(mla_new.shape, BF16),
             pltpu.VMEM(w_uk.shape, BF16),
-            pltpu.VMEM(w_uv.shape, BF16),
+            pltpu.VMEM((latent, heads * hd), BF16),
             pltpu.VMEM((2 * heads, lanes), jnp.int32),
             pltpu.VMEM(page_table.shape[1:], jnp.int32),
             pltpu.VMEM((2, lanes), jnp.int32),
@@ -626,7 +633,7 @@
             pltpu.VMEM((4 * n_dp, hd, hd), BF16),
             pltpu.VMEM((rows, heads, tokens, latent), BF16),
             pltpu.VMEM((n_t, heads, tokens, latent), BF16),
-            pltpu.VMEM((n_t, heads, latent, hd), BF16),
+            pltpu.VMEM((n_t, latent, heads * hd), BF16),
             pltpu.VMEM((rows, pages_row * page_len, latent), BF16),
             pltpu.VMEM((n_t + 1, pages_row * page_len, latent), BF16),
             pltpu.VMEM((n_t, tokens, heads * hd), BF16),
@@ -640,7 +647,7 @@
             dma((2, max(n_z, n_y))),
         ]
         + [dma((n_t,))] * 8
-        + [dma((heads + latent // hd,)), dma((9,)), dma((4,))],
+        + [dma((heads + latent // hd,)), dma((8 + heads,)), dma((4,))],
         compiler_params=pltpu.CompilerParams(
             collective_id=0, has_side_effects=True, vmem_limit_bytes=60 * 1024 * 1024
         ),

time: 130 us -> 131 us (level)
  no operation moved by 1% of the time
where the time goes in v6:
time: 131 us
  Pallas kernels  129 us (98%)
    pallas_call x1, Pallas kernels, run_fused(): pl.pallas_call(functools.partial(fused, sizes), out_shape=out, in_specs=[...  129 us

profile of v6, /device:TPU:1, one launch (start us, length us, event | category | flops | bytes accessed | tf_op | source)
XLA Modules:
  0.0 130.6 jit_solution(3143384058994489288)
XLA Ops:
  0.6 129.1 %shard_map.149 = bf16[2,8,32,512]{3,2,1,0:T(8,128)(2,1)S(1)} custom-call(s32[8]{0:T(128)} %len_ref.1, s32[32,512]{1,0:T(8,128)} %bitcast.7, s32[8,4,512]{2,1,0:T(4,128)} %bitcast.8, bf16[4,8,128,128]{3,2,1,0:T(8,128)(2,1)} %states_ref.1, bf16[1,32,32,512]{3,2,1,0:T(8,128)(2,1)} %pages_ref.1, bf16[8,32,512]{2,1,0:T(8,128)(2,1)} %q_ref.1, ...), custom_call_target="tpu_custom_call" | custom-call | tf_op jit(solution)/shard_map/pallas_call | solution.py:610
  129.7 0.8 slice_bitcast_fusion

commit v7 on v6

--- a/solution.py
+++ b/solution.py
@@ -429,8 +429,8 @@
         return c
 
     def work(i, c):
-        make_coefficients(i - 1, c)
-        return pass_on(i, c)
+        pass_on(i, c)
+        return make_coefficients(i - 1, c)
 
     assert n_z == n_y
     paired = min(rows, n_z - 1)
@@ -461,8 +461,14 @@
         return c
 
     pages_row = page_out.shape[1] // page_len
-    lax.fori_loop(0, rows * pages_row, place_page, 0)
-    context[0] = page_out[mine]
+
+    def place_row_of(r):
+        lax.fori_loop(0, pages_row, lambda j, c: place_page(r * pages_row + j, c), 0)
+
+    def hand_over(k):
+        place_row_of((mine + k) % n_t)
+        page_copy(k).start()
+
     odd = mine % 2
     twin = 1 + (n_t - 2) * odd
     far = n_t // 4
@@ -471,10 +477,12 @@
     def cores(p):
         return (2 * p - odd, 2 * p + 1 - odd)
 
-    page_copy(twin).start()
+    hand_over(twin)
     for p in near_chips + [far]:
         for k in cores(p):
-            page_copy(k).start()
+            hand_over(k)
+    place_row_of(mine)
+    context[0] = page_out[mine]
 
     def recall(r, c):
         alive = (lax.broadcasted_iota(jnp.int32, (tokens, 1), 0) < len_ref[r]).astype(F32)

time: 131 us -> 130 us (level)
  no operation moved by 1% of the time
where the time goes in v7:
time: 130 us
  Pallas kernels  129 us (99%)
    pallas_call x1, Pallas kernels, run_fused(): pl.pallas_call(functools.partial(fused, sizes), out_shape=out, in_specs=[...  129 us

profile of v7, /device:TPU:1, one launch (start us, length us, event | category | flops | bytes accessed | tf_op | source)
XLA Modules:
  0.0 130.2 jit_solution(13480601653897778653)
XLA Ops:
  0.6 128.8 %shard_map.149 = bf16[2,8,32,512]{3,2,1,0:T(8,128)(2,1)S(1)} custom-call(s32[8]{0:T(128)} %len_ref.1, s32[32,512]{1,0:T(8,128)} %bitcast.7, s32[8,4,512]{2,1,0:T(4,128)} %bitcast.8, bf16[4,8,128,128]{3,2,1,0:T(8,128)(2,1)} %states_ref.1, bf16[1,32,32,512]{3,2,1,0:T(8,128)(2,1)} %pages_ref.1, bf16[8,32,512]{2,1,0:T(8,128)(2,1)} %q_ref.1, ...), custom_call_target="tpu_custom_call" | custom-call | tf_op jit(solution)/shard_map/pallas_call | solution.py:618
  129.4 0.8 slice_bitcast_fusion
